TPU v7x, 512 devices: a whole 4x8x8 slice. The times are simulated.
512 devices in a mesh: gx: 16 (over x, y_lo), gy: 32 (over y_hi, z, core).
Axes of the slice: x: 4, y: 8 (y_hi: 2, y_lo: 4; y = y_hi * 4 + y_lo), z: 8, core: 2. Of those that a mesh axis runs over, the one named last changes fastest.
Arguments:
- start_block: float32 [16, 16, 32, 64, 128], P(None, 'gx', 'gy'), may hold values from -4 to 4
- labels: int32 [16, 32, 64, 128], P('gx', 'gy'), may hold values from -8 to 15
- materials: int32 [16, 32, 128], P('gx', 'gy'), may hold values from 0 to 7
- mat_scales: float32 [8], replicated, may hold values from 0.01 to 0.1
- cell_stiffness: float32 [125, 125], replicated, may hold values from -16 to 16, as said below
Outputs:
- solution: float32 [16, 16, 32, 64, 128], P(None, 'gx', 'gy')
- residual: float32 [16, 16, 32, 64, 128], P(None, 'gx', 'gy')
Inputs may be any that keep to these rules, and one draw needn't show every extreme that they name: `labels`: a label c of 0 or more puts the node on conductor c; a negative label puts it on none. `materials`: an index into mat_scales. `cell_stiffness`: symmetric positive semidefinite, every row sums to zero.
All inputs are finite; a program needn't handle non-finite values.
Results may differ from a plain program's by a relative error of at most 0.002.
Values sent between devices are 32-bit elements; how exact they have to be, the bound alone decides.
A program may use at most 64 MiB of HBM per device.

v0:
```python
import jax
import jax.numpy as jnp
from jax import lax
from jax.sharding import PartitionSpec as P

ITERS = 4


PENALTY = 1.0


def passed_along(value, axis, steps):
    count = lax.axis_size(axis)
    pairs = [(source, (source + steps) % count) for source in range(count)]
    return lax.ppermute(value, axis, pairs)


def from_behind(value, axis, steps):
    count = lax.axis_size(axis)
    first, last = (max(0, -steps), min(count, count - steps))
    return lax.ppermute(value, axis, [(source, source + steps) for source in range(first, last)])


def next_plane(values):
    return jnp.concatenate([values[..., 1:], jnp.zeros_like(values[..., :1])], -1)


def prev_plane(values):
    return jnp.concatenate([jnp.zeros_like(values[..., :1]), values[..., :-1]], -1)


def assemble(picker):
    slabs = []
    for along_x in range(5):
        for along_y in range(5):
            four = picker(along_x, along_y)
            slabs.append(four)
            slabs.append(next_plane(four[..., 0:1, :]))
    return jnp.concatenate(slabs, 3)


def fold_planes(mapped):
    slabs = []
    for along_x in range(5):
        for along_y in range(5):
            start = 25 * along_x + 5 * along_y
            four = mapped[..., start : start + 4, :]
            last = mapped[..., start + 4 : start + 5, :]
            slabs.append(four[..., 0:1, :] + prev_plane(last))
            slabs.append(four[..., 1:4, :])
    return jnp.concatenate(slabs, 3)


def extend_rims(field):
    east = passed_along(field[:, :1, :, 0:16], "gx", -1)
    nextx = jnp.concatenate([field[:, 1:, :, 0:16], east], 1)
    wider = jnp.concatenate([field, nextx], 3)
    lower = jnp.concatenate(
        [wider[..., 16 * along_x : 16 * along_x + 4, :] for along_x in range(5)], 3
    )
    north = from_behind(lower, "gy", -1)
    next_rows = jnp.concatenate([lower[:, :, 1:], north], 2)

    def picker(along_x, along_y):
        if along_y < 4:
            start = 16 * along_x + 4 * along_y
            return wider[..., start : start + 4, :]
        return next_rows[..., 4 * along_x : 4 * along_x + 4, :]

    return assemble(picker)


def return_rims(folded):
    upper = jnp.concatenate(
        [folded[..., 20 * along_x + 16 : 20 * along_x + 20, :] for along_x in range(5)], 3
    )
    inner = jnp.concatenate(
        [folded[..., 20 * along_x : 20 * along_x + 16, :] for along_x in range(5)], 3
    )
    below = from_behind(upper, "gy", 1)
    moved = jnp.concatenate([below, upper[:, :, :-1]], 2)
    filler = jnp.zeros_like(inner[..., 0:12, :])
    inner = inner + jnp.concatenate(
        [
            piece
            for along_x in range(5)
            for piece in (moved[..., 4 * along_x : 4 * along_x + 4, :], filler)
        ],
        3,
    )
    outer = inner[..., 64:80, :]
    core = inner[..., 0:64, :]
    behind = passed_along(outer, "gx", 1)
    movedx = jnp.concatenate([behind, outer[:, :-1]], 1)
    return core + jnp.concatenate([movedx, jnp.zeros_like(core[..., 16:64, :])], 3)


def gram(left, right):
    columns = left.shape[0]
    return jnp.dot(
        left.reshape(columns, -1), right.reshape(columns, -1).T, precision=lax.Precision.HIGHEST
    )


def combine(coef, block):
    columns = block.shape[0]
    return jnp.dot(coef.T, block.reshape(columns, -1), precision=lax.Precision.HIGHEST).reshape(
        block.shape
    )


def solve_spd(matrix, rhs):
    factor = jnp.linalg.cholesky(matrix)
    return jax.scipy.linalg.cho_solve((factor, True), rhs, check_finite=False)


def on_device(start_block, labels, materials, mat_scales, cell_stiffness):
    columns = start_block.shape[0]
    mask = (labels >= 0).astype(jnp.float32)
    targets = (
        labels[None] == jnp.arange(columns, dtype=jnp.int32)[:, None, None, None, None]
    ).astype(jnp.float32)
    scales = jnp.zeros(materials.shape, jnp.float32)
    for which in range(mat_scales.shape[0]):
        scales = scales + jnp.where(materials == which, mat_scales[which], 0.0)

    def operate(field):
        expanded = extend_rims(field)
        mapped = jnp.einsum(
            "pq,cijqk->cijpk", cell_stiffness, expanded, precision=lax.Precision.HIGHEST
        )
        mapped = mapped * scales[None, :, :, None, :]
        return return_rims(fold_planes(mapped)) + PENALTY * mask[None] * field

    solution = start_block
    residual = targets - operate(start_block)
    direction = residual
    norm_now = lax.psum(gram(residual, residual), ("gx", "gy"))
    for step in range(ITERS):
        image = operate(direction)
        curv = lax.psum(gram(direction, image), ("gx", "gy"))
        alpha = solve_spd(curv, norm_now)
        solution = solution + combine(alpha, direction)
        residual = residual - combine(alpha, image)
        if step + 1 < ITERS:
            norm_next = lax.psum(gram(residual, residual), ("gx", "gy"))
            beta = solve_spd(norm_now, norm_next)
            direction = residual + combine(beta, direction)
            norm_now = norm_next
    return (solution, residual)


def solution(mesh):
    return jax.shard_map(
        on_device,
        mesh=mesh,
        in_specs=(
            P(None, "gx", "gy", None, None),
            P("gx", "gy", None, None),
            P("gx", "gy", None),
            P(),
            P(),
        ),
        out_specs=(P(None, "gx", "gy", None, None), P(None, "gx", "gy", None, None)),
        check_vma=False,
    )
```

profile of v0, /device:TPU:1, one launch (start us, length us, event | category | flops | bytes accessed | tf_op | source)
XLA Modules:
  0.0 1192.1 jit_solution(5960313065019231316)
XLA Ops:
  1.6 8.3 collective-permute-start
  13.8 5.1 fusion.114
  19.0 2.9 collective-permute-start.1
  22.1 5.1 collective-permute-done.1
  27.4 2.2 concatenate.1038
  31.5 1.9 collective-permute-start.2
  37.1 1.9 collective-permute-start.3
  39.0 8.6 collective-permute-done.3
  56.5 1.9 collective-permute-start.4
  58.5 4.7 collective-permute-done.4
  64.0 3.0 collective-permute-start.5
  69.5 3.0 collective-permute-done.5
  73.8 2.2 concatenate.1095
  76.0 1.7 fusion.3
  79.7 2.1 collective-permute-start.6
  86.2 1.9 collective-permute-start.7
  89.1 7.5 collective-permute-done.7
  97.9 112.7 %all-reduce.255 = (f32[16,16]{0,1:T(8,128)S(1)}, f32[16,16]{0,1:T(8,128)S(1)}) all-reduce(f32[16,16]{0,1:T(8,128)S(1)} %convolution_bitcast_fusion.22, f32[16,16]{0,1:T(8,128)S(1)} %convolution_bitcast_fusion.23), channel_id=1, replica_groups=mesh['gx'=16,'gy'=32] {'gx','gy'}, use_global_device_ids=true, to_apply=%region_3.5 | all-reduce | flops 512 | bytes 4096 | tf_op jit(solution)/shard_map/psum | solution.py:138
  221.2 95.1 %psum.58 = f32[16,16]{0,1:T(8,128)S(1)} all-reduce(f32[16,16]{0,1:T(8,128)S(1)} %convolution_bitcast_fusion.20), channel_id=1, replica_groups=mesh['gx'=16,'gy'=32] {'gx','gy'}, use_global_device_ids=true, to_apply=%region_4.7 | all-reduce | flops 256 | bytes 2048 | tf_op jit(solution)/shard_map/psum | solution.py:146
  319.8 7.0 collective-permute-start.8
  337.9 3.3 collective-permute-start.9
  346.8 33.5 %concatenate.1151 = f32[16,1,1,125,128]{4,3,0,2,1:T(8,128)} concatenate(f32[16,1,1,4,128]{4,3,0,2,1:T(4,128)S(1)} %get-tuple-element.480, f32[16,1,1,1,128]{4,3,0,2,1:T(1,128)S(1)} %copy-done.52, f32[16,1,1,4,128]{4,3,0,2,1:T(4,128)S(1)} %get-tuple-element.479, f32[16,1,1,1,128]{4,3,0,2,1:T(1,128)S(1)} %copy-done.51, f32[16,1,1,4,128]{4,3,0,2,1:T(4,128)S(1)} %get-tuple-element.478, ...), dimensions={3} | concatenate | bytes 2048000 | tf_op jit(solution)/shard_map/concatenate | solution.py:39
  380.2 2.3 fusion.5
  385.3 1.9 collective-permute-start.10
  387.2 2.0 slice_add_fusion.64
  389.2 1.8 slice_add_fusion.73
  391.0 8.4 concatenate.1172
  399.5 11.3 concatenate.1179
  412.7 1.9 collective-permute-start.11
  416.6 6.5 collective-permute-done.11
  425.4 98.5 %psum.59 = f32[16,16]{0,1:T(8,128)S(1)} all-reduce(f32[16,16]{0,1:T(8,128)S(1)} %convolution_bitcast_fusion.18), channel_id=1, replica_groups=mesh['gx'=16,'gy'=32] {'gx','gy'}, use_global_device_ids=true, to_apply=%region_5.8 | all-reduce | flops 256 | bytes 2048 | tf_op jit(solution)/shard_map/psum | solution.py:141
  530.6 95.5 %psum.60 = f32[16,16]{0,1:T(8,128)S(1)} all-reduce(f32[16,16]{0,1:T(8,128)S(1)} %convolution_bitcast_fusion.16), channel_id=1, replica_groups=mesh['gx'=16,'gy'=32] {'gx','gy'}, use_global_device_ids=true, to_apply=%region_6.9 | all-reduce | flops 256 | bytes 2048 | tf_op jit(solution)/shard_map/psum | solution.py:146
  630.8 1.8 custom-call.18
  642.3 2.8 collective-permute-start.12
  645.8 2.7 collective-permute-done.12
  649.2 2.0 concatenate.1185
  651.1 3.4 collective-permute-start.13
  663.3 37.9 %concatenate.1207 = f32[16,1,1,125,128]{4,3,0,2,1:T(8,128)} concatenate(f32[16,1,1,4,128]{4,3,0,2,1:T(4,128)S(1)} %get-tuple-element.448, f32[16,1,1,1,128]{4,3,0,2,1:T(1,128)} %concatenate.1181, f32[16,1,1,4,128]{4,3,0,2,1:T(4,128)} %get-tuple-element.447, f32[16,1,1,1,128]{4,3,0,2,1:T(1,128)} %concatenate.1182, f32[16,1,1,4,128]{4,3,0,2,1:T(4,128)S(1)} %copy-done.13, ...), dimensions={3} | concatenate | bytes 2048000 | tf_op jit(solution)/shard_map/concatenate | solution.py:39
  701.2 2.3 fusion.7
  706.2 2.0 concatenate.1234
  708.2 1.9 collective-permute-start.14
  710.1 2.0 slice_add_fusion.39
  712.1 1.8 slice_add_fusion.48
  713.9 8.6 concatenate.1228
  724.1 14.3 %concatenate.1235 = f32[16,1,1,80,128]{4,3,0,2,1:T(8,128)} concatenate(f32[16,1,1,4,128]{4,3,0,2,1:T(4,128)} %get-tuple-element.564, f32[16,1,1,12,128]{4,3,0,2,1:T(8,128)S(1)} %concatenate.1066, f32[16,1,1,4,128]{4,3,0,2,1:T(4,128)} %get-tuple-element.563, f32[16,1,1,12,128]{4,3,0,2,1:T(8,128)S(1)} %concatenate.1066, f32[16,1,1,4,128]{4,3,0,2,1:T(4,128)} %get-tuple-element.562, ...), dimensions={3} | concatenate | bytes 1310720 | tf_op jit(solution)/shard_map/concatenate | solution.py:83
  739.6 2.1 collective-permute-start.15
  743.3 5.9 collective-permute-done.15
  750.5 101.2 %psum.61 = f32[16,16]{0,1:T(8,128)S(1)} all-reduce(f32[16,16]{0,1:T(8,128)S(1)} %convolution_bitcast_fusion.14), channel_id=1, replica_groups=mesh['gx'=16,'gy'=32] {'gx','gy'}, use_global_device_ids=true, to_apply=%region_7.10 | all-reduce | flops 256 | bytes 2048 | tf_op jit(solution)/shard_map/psum | solution.py:141
  858.2 95.3 %psum.62 = f32[16,16]{1,0:T(8,128)S(1)} all-reduce(f32[16,16]{1,0:T(8,128)S(1)} %convolution_bitcast_fusion.12), channel_id=1, replica_groups=mesh['gx'=16,'gy'=32] {'gx','gy'}, use_global_device_ids=true, to_apply=%region_8.11 | all-reduce | flops 256 | bytes 2048 | tf_op jit(solution)/shard_map/psum | solution.py:146
  965.5 2.8 collective-permute-start.16
  969.1 2.6 collective-permute-done.16
  972.4 2.0 concatenate.1241
  974.4 3.4 collective-permute-start.17
  985.7 38.1 %concatenate.1263 = f32[16,1,1,125,128]{4,3,0,2,1:T(8,128)} concatenate(f32[16,1,1,4,128]{4,3,0,2,1:T(4,128)S(1)} %get-tuple-element.416, f32[16,1,1,1,128]{4,3,0,2,1:T(1,128)} %concatenate.1237, f32[16,1,1,4,128]{4,3,0,2,1:T(4,128)} %get-tuple-element.415, f32[16,1,1,1,128]{4,3,0,2,1:T(1,128)} %concatenate.1238, f32[16,1,1,4,128]{4,3,0,2,1:T(4,128)} %get-tuple-element.414, ...), dimensions={3} | concatenate | bytes 2048000 | tf_op jit(solution)/shard_map/concatenate | solution.py:39
  1023.8 2.3 fusion.9
  1030.0 4.4 concatenate.1290
  1034.4 1.9 collective-permute-start.18
  1037.1 2.0 slice_add_fusion.14
  1039.8 1.8 slice_add_fusion.23
  1041.6 14.7 %concatenate.1284 = f32[16,1,1,80,128]{4,3,0,2,1:T(8,128)} concatenate(f32[16,1,1,1,128]{4,3,0,2,1:T(1,128)} %get-tuple-element.72, f32[16,1,1,3,128]{4,3,0,2,1:T(4,128)} %get-tuple-element.78, f32[16,1,1,1,128]{4,3,0,2,1:T(1,128)} %get-tuple-element.71, f32[16,1,1,3,128]{4,3,0,2,1:T(4,128)S(1)} %get-tuple-element.77, f32[16,1,1,1,128]{4,3,0,2,1:T(1,128)} %get-tuple-element.70, ...), dimensions={3} | concatenate | bytes 1310720 | tf_op jit(solution)/shard_map/concatenate | solution.py:77
  1057.3 11.3 concatenate.1291
  1070.0 2.4 collective-permute-start.19
  1074.0 5.6 collective-permute-done.19
  1081.0 101.0 %psum.63 = f32[16,16]{0,1:T(8,128)S(1)} all-reduce(f32[16,16]{0,1:T(8,128)S(1)} %convolution_bitcast_fusion.10), channel_id=1, replica_groups=mesh['gx'=16,'gy'=32] {'gx','gy'}, use_global_device_ids=true, to_apply=%region_9.12 | all-reduce | flops 256 | bytes 2048 | tf_op jit(solution)/shard_map/psum | solution.py:141
  (495 shorter events, 159.3 us)
Async XLA Ops:
  0.6 29.0 %copy-start = (f32[125,125]{1,0:T(8,128)S(1)}, f32[125,125]{1,0:T(8,128)}, u32[]{:S(2)}) copy-start(f32[125,125]{1,0:T(8,128)} %param.12) | copy-start | bytes 187504
  0.6 10.9 copy-start.1
  1.6 17.2 %collective-permute-start = (f32[16,1,1,16,128]{4,3,0,2,1:T(8,128)S(1)}, f32[16,1,1,16,128]{4,3,0,2,1:T(8,128)S(1)}, u32[]{:S(2)}, u32[]{:S(2)}) collective-permute-start(f32[16,1,1,16,128]{4,3,0,2,1:T(8,128)S(1)} %slice.3830), channel_id=1, source_target_pairs={{0,480},{32,0},{64,32},{96,64},{128,96},{160,128},{192,160},{224,1... | collective-permute-start | bytes 393224 | tf_op jit(solution)/shard_map/ppermute | solution.py:15
  18.8 10.8 copy-start.83
  19.0 8.2 collective-permute-start.1
  31.5 4.5 collective-permute-start.2
  37.0 2.0 copy-start.14
  37.1 10.5 collective-permute-start.3
  56.5 6.7 collective-permute-start.4
  64.0 8.5 collective-permute-start.5
  72.9 0.8 copy-start.55
  72.9 0.8 copy-start.57
  73.0 0.8 copy-start.59
  73.0 0.8 copy-start.15
  79.7 5.5 collective-permute-start.6
  82.5 1.1 copy-start.70
  82.5 1.1 copy-start.71
  82.5 1.1 copy-start.72
  82.5 1.1 copy-start.73
  82.5 1.1 copy-start.74
  82.6 1.1 copy-start.81
  86.2 10.4 collective-permute-start.7
  319.8 7.6 copy-start.66
  319.8 17.3 %collective-permute-start.8 = (f32[16,1,1,16,128]{4,3,0,2,1:T(8,128)S(1)}, f32[16,1,1,16,128]{4,3,0,2,1:T(8,128)S(1)}, u32[]{:S(2)}, u32[]{:S(2)}) collective-permute-start(f32[16,1,1,16,128]{4,3,0,2,1:T(8,128)S(1)} %slice.4096), channel_id=1, source_target_pairs={{0,480},{32,0},{64,32},{96,64},{128,96},{160,128},{192,160},{224,1... | collective-permute-start | bytes 393224 | tf_op jit(solution)/shard_map/ppermute | solution.py:15
  337.9 7.0 collective-permute-start.9
  345.8 0.8 copy-start.47
  345.8 0.8 copy-start.48
  345.9 0.8 copy-start.50
  345.9 0.8 copy-start.51
  345.9 0.8 copy-start.52
  345.9 0.8 copy-start.54
  345.9 0.8 copy-start.56
  345.9 0.8 copy-start.58
  346.0 0.8 copy-start.17
  346.8 33.5 %copy-start.84 = (f32[128]{0:T(128)S(1)}, f32[128]{0:T(128)}, u32[]{:S(2)}) copy-start(f32[128]{0:T(128)} %copy-done.83) | copy-start | bytes 1540
  382.5 2.6 copy-start.3
  385.3 14.1 %collective-permute-start.10 = (f32[16,1,1,20,128]{4,3,0,2,1:T(8,128)S(1)}, f32[16,1,1,20,128]{4,3,0,2,1:T(8,128)S(1)}, u32[]{:S(2)}, u32[]{:S(2)}) collective-permute-start(f32[16,1,1,20,128]{4,3,0,2,1:T(8,128)S(1)} %concatenate.1178), channel_id=1, source_target_pairs={{0,1},{1,2},{2,3},{3,4},{4,5},{5,6},{6,7},{7,8},{8,9},{9,10},{10,1... | collective-permute-start | bytes 491528 | tf_op jit(solution)/shard_map/ppermute | solution.py:21
  411.9 0.8 copy-start.5
  412.7 1.9 copy-start.67
  412.7 10.4 collective-permute-start.11
  528.5 0.8 copy-start.19
  642.3 6.2 collective-permute-start.12
  651.1 7.5 collective-permute-start.13
  661.8 0.8 copy-start.13
  663.3 37.9 %copy-start.85 = (f32[128]{0:T(128)S(1)}, f32[128]{0:T(128)}, u32[]{:S(2)}) copy-start(f32[128]{0:T(128)} %copy-done.83) | copy-start | bytes 1540
  703.5 2.7 copy-start.4
  708.2 14.3 %collective-permute-start.14 = (f32[16,1,1,20,128]{4,3,0,2,1:T(8,128)}, f32[16,1,1,20,128]{4,3,0,2,1:T(8,128)}, u32[]{:S(2)}, u32[]{:S(2)}) collective-permute-start(f32[16,1,1,20,128]{4,3,0,2,1:T(8,128)} %concatenate.1234), channel_id=1, source_target_pairs={{0,1},{1,2},{2,3},{3,4},{4,5},{5,6},{6,7},{7,8},{8,9},{9,10},{10,1... | collective-permute-start | bytes 491528 | tf_op jit(solution)/shard_map/ppermute | solution.py:21
  739.6 2.2 copy-start.20
  739.6 9.6 collective-permute-start.15
  858.2 95.3 %copy-start.65 = (f32[1,16,16]{1,2,0:T(8,128)S(1)}, f32[1,16,16]{1,2,0:T(8,128)}, u32[]{:S(2)}) copy-start(f32[1,16,16]{1,2,0:T(8,128)} %custom-call.18) | copy-start | bytes 3076
  965.5 6.2 collective-permute-start.16
  974.4 7.5 collective-permute-start.17
  1026.1 3.9 copy-start.2
  1034.4 21.9 %collective-permute-start.18 = (f32[16,1,1,20,128]{4,3,0,2,1:T(8,128)}, f32[16,1,1,20,128]{4,3,0,2,1:T(8,128)}, u32[]{:S(2)}, u32[]{:S(2)}) collective-permute-start(f32[16,1,1,20,128]{4,3,0,2,1:T(8,128)} %concatenate.1290), channel_id=1, source_target_pairs={{0,1},{1,2},{2,3},{3,4},{4,5},{5,6},{6,7},{7,8},{8,9},{9,10},{10,1... | collective-permute-start | bytes 491528 | tf_op jit(solution)/shard_map/ppermute | solution.py:21
  1037.0 2.1 copy-start.76
  1037.0 2.1 copy-start.77
  1037.0 2.1 copy-start.78
  1037.0 2.1 copy-start.79
  1037.1 2.1 copy-start.80
  1037.1 2.1 copy-start.82
  1070.0 9.6 collective-permute-start.19
  1184.2 1.9 copy-start.22
  1188.4 1.0 copy-start.6
  1188.4 1.2 copy-start.7
  (43 other events, 32.0 us)
where the time goes:
time: 1210 us; the launch traced here: 1190 us
  blocking collectives  699 us (58%)
  local copies, waits for them, and re-layouts  284 us (23%)
  starting transfers between devices  58.7 us (5%)
  other arithmetic  57.8 us (5%)
  waiting for transfers between devices  57 us (5%)
  matrix products  32.1 us (3%)
    psum x3, blocking collectives, on_device(): curv = lax.psum(gram(direction, image), ('gx', 'gy'))  301 us
    psum x3, blocking collectives, on_device(): norm_next = lax.psum(gram(residual, residual), ('gx', 'gy'))  286 us
    concatenate x5, local copies, waits for them, and re-layouts, assemble(): return jnp.concatenate(slabs, 3)  114 us
    psum x1, blocking collectives, on_device(): norm_now = lax.psum(gram(residual, residual), ('gx', 'gy'))  113 us
    concatenate x125, local copies, waits for them, and re-layouts, next_plane(): jnp.concatenate([values[..., 1:], jnp.zeros_like(values[..., :1])], -1)  53.9 us
    ppermute x10, waiting for transfers between devices, passed_along(): return lax.ppermute(value, axis, pairs)  44.1 us
    concatenate x6, local copies, waits for them, and re-layouts, return_rims(): jnp.concatenate([piece for along_x in range(5) for piece in (moved[..., 4...  38.7 us
    concatenate x5, local copies, waits for them, and re-layouts, return_rims(): jnp.concatenate([folded[..., 20 * along_x:20 * along_x + 16, :] for along...  33 us
  transfers between devices with their start and end apart: 20, of which 14 were waited for; matrix products, arithmetic and copies ran while one was open for 7% of the time, Pallas kernels for 0%

commit v1 on v0

v1 whole, which is shorter than its diff:
```python
import functools

import jax
import jax.numpy as jnp
import ml_dtypes
import numpy as np
from jax import lax
from jax.experimental import pallas as pl
from jax.experimental.pallas import tpu as pltpu
from jax.sharding import PartitionSpec as P

COLS = 16
NQ = 4
CQ = COLS // NQ
PENALTY = 1.0
MESH = pl.DeviceIdType.MESH
BF = jnp.bfloat16
F32 = jnp.float32


def node_order():
    rows = [(a, b, d) for a in range(4) for b in range(4) for d in range(4)]
    rows += [(4, b, d) for b in range(4) for d in range(4)]
    rows += [(a, 4, d) for a in range(4) for d in range(4)]
    rows += [(a, b, 4) for a in range(4) for b in range(4)]
    rows += [(4, b, 4) for b in range(4)]
    rows += [(a, 4, 4) for a in range(4)]
    rows += [(4, 4, d) for d in range(5)]
    return [25 * a + 5 * b + d for a, b, d in rows]


def order_matrix():
    out = np.zeros((128, 128), np.float32)
    for row, node in enumerate(node_order()):
        out[row, node] = 1.0
    return out.astype(ml_dtypes.bfloat16)


def moment_tables():
    mu = np.zeros((8, 8))
    for k in range(4):
        mu[k, k] = 1.0
    mu[4, 4] = 1.0
    for i in (1, 2, 3):
        mu[4 + i, 4 + i] = 2.0
        mu[4 + i] -= mu[4 - i]

    def inner(i, j):
        return 0.5 * (mu[i + j] + mu[abs(i - j)])

    tables = np.zeros((3, 4, 8, 8))
    for i in range(4):
        for j in range(4):
            tables[0, i, :, j] = inner(i, j)
            tables[1, i, :, j] = 0.5 * (inner(i, j + 1) + inner(i, abs(j - 1)))
        tables[2, i, :, 4] = inner(i, 0)
    out = np.zeros((128, 3 * 4 * 128), np.float32)
    for which in range(3):
        for i in range(4):
            start = 128 * (4 * which + i)
            out[:, start : start + 128] = np.kron(tables[which, i], np.eye(16))
    return out.astype(ml_dtypes.bfloat16)


def split(value):
    high = value.astype(BF)
    low = (value - high.astype(F32)).astype(BF)
    return high, low


def dot(left, right):
    return jnp.dot(left, right, preferred_element_type=F32)


def dot_t(left, right):
    return lax.dot_general(left, right, (((1,), (1,)), ((), ())), preferred_element_type=F32)


def exact_dot(value, table):
    rows = value.shape[0]
    high = value.astype(BF)
    rest = value - high.astype(F32)
    middle = rest.astype(BF)
    low = (rest - middle.astype(F32)).astype(BF)
    out = dot(jnp.concatenate([high, middle, low], 0), table)
    return out[0:rows] + out[rows : 2 * rows] + out[2 * rows : 3 * rows]


def iota(shape, axis):
    return lax.broadcasted_iota(jnp.int32, shape, axis)


def ones_where(condition):
    return jnp.where(condition, 1.0, 0.0).astype(BF)


def kernel(
    nx, ny, n1,
    x0, lab, mat, ms, kin, order, table,
    xo, ro,
    v, w, rim, corner, ysend, csend, zs, zcs, zr, zcr, tail, kpad, kk, klo, maskb, srow,
    stat, stbuf, gbuf, gm, yst, gres, colr, cs_ref,
    es, er, rs, rr, ss, sr,
):
    gx = lax.axis_index("gx")
    gy = lax.axis_index("gy")
    n3 = ny // n1
    xprev = lax.rem(gx + nx - 1, nx)
    xnext = lax.rem(gx + 1, nx)
    has_prev = gy > 0
    has_next = gy < ny - 1
    yprev = lax.max(gy - 1, 0)
    ynext = lax.min(gy + 1, ny - 1)

    pos1 = lax.rem(gy, n1)
    pos3 = lax.div(gy, n1)
    stages = (
        (0, n1, pos1, lambda p: (gx, gy - pos1 + p)),
        (n1, nx, gx, lambda p: (p, gy)),
        (n1 + nx, n3, pos3, lambda p: (gx, p * n1 + pos1)),
    )

    barrier = pltpu.get_barrier_semaphore()

    def greet(device):
        pl.semaphore_signal(barrier, inc=1, device_id=device, device_id_type=MESH)

    greet((xprev, gy))
    greet((xnext, gy))

    @pl.when(has_prev)
    def _():
        greet((gx, yprev))
        greet((xprev, yprev))

    @pl.when(has_next)
    def _():
        greet((gx, ynext))
        greet((xnext, ynext))

    for _, size, pos, device in stages:
        def hello(i, carry, size=size, pos=pos, device=device):
            greet(device(lax.rem(pos + i, size)))
            return carry

        lax.fori_loop(1, size, hello, 0)

    kpad[...] = jnp.zeros_like(kpad)
    kpad[0:125, 0:125] = kin[...]
    khigh, klow = split(kpad[...])
    pm = order[...]

    def permuted(value):
        return dot_t(dot(pm, value).astype(BF), pm).astype(BF)

    khigh = permuted(khigh)
    kk[:, 0:128] = khigh
    kk[:, 128:256] = khigh
    klo[...] = permuted(klow)
    maskb[...] = jnp.where(lab[...] >= 0, PENALTY, 0.0)
    scale = jnp.zeros((1, 128), F32)
    for which in range(8):
        scale = scale + jnp.where(mat[...] == which, ms[which], 0.0)
    srow[...] = jnp.broadcast_to(scale, (8, 128))
    tail[...] = jnp.zeros_like(tail)

    @pl.when(jnp.logical_not(has_next))
    def _():
        rim[:, :, 16:32, :] = jnp.zeros((NQ, CQ, 16, 128), F32)
        corner[...] = jnp.zeros_like(corner)

    @pl.when(jnp.logical_not(has_prev))
    def _():
        zr[:, :, 16:32, :] = jnp.zeros((NQ, CQ, 16, 128), F32)
        zcr[...] = jnp.zeros_like(zcr)

    def rcopy(src, dst, send, recv, device):
        return pltpu.make_async_remote_copy(
            src_ref=src, dst_ref=dst, send_sem=send, recv_sem=recv, device_id=device, device_id_type=MESH
        )

    def ext(src, q):
        first = pl.ds(0, 16)
        return (
            rcopy(src.at[q, :, first], rim.at[q, :, first], es.at[0, q], er.at[0, q], (xprev, gy)),
            rcopy(ysend.at[q], rim.at[q, :, pl.ds(16, 16)], es.at[1, q], er.at[1, q], (gx, yprev)),
            rcopy(csend.at[q], corner.at[q], es.at[2, q], er.at[2, q], (xprev, yprev)),
        )

    def ret(q):
        first, second = pl.ds(0, 16), pl.ds(16, 16)
        return (
            rcopy(zs.at[q, :, first], zr.at[q, :, first], rs.at[0, q], rr.at[0, q], (xnext, gy)),
            rcopy(zs.at[q, :, second], zr.at[q, :, second], rs.at[1, q], rr.at[1, q], (gx, ynext)),
            rcopy(zcs.at[q], zcr.at[q], rs.at[2, q], rr.at[2, q], (xnext, ynext)),
        )

    def extend_start(src, q):
        for j in range(CQ):
            for a in range(4):
                ysend[q, j, 4 * a : 4 * a + 4, :] = src[q, j, 16 * a : 16 * a + 4, :]
            csend[q, 4 * j : 4 * j + 4, :] = src[q, j, 0:4, :]
        copies = ext(src, q)
        copies[0].start()

        @pl.when(has_prev)
        def _():
            copies[1].start()
            copies[2].start()

    def extend_arrived(src, q):
        copies = ext(src, q)
        copies[0].wait_recv()

        @pl.when(has_next)
        def _():
            copies[1].wait_recv()
            copies[2].wait_recv()

    def extend_sent(src, q):
        copies = ext(src, q)
        copies[0].wait_send()

        @pl.when(has_prev)
        def _():
            copies[1].wait_send()
            copies[2].wait_send()

    def return_start(q):
        copies = ret(q)
        copies[0].start()

        @pl.when(has_next)
        def _():
            copies[1].start()
            copies[2].start()

    def return_arrived(q):
        copies = ret(q)
        copies[0].wait_recv()

        @pl.when(has_prev)
        def _():
            copies[1].wait_recv()
            copies[2].wait_recv()

    def return_sent(q):
        copies = ret(q)
        copies[0].wait_send()

        @pl.when(has_next)
        def _():
            copies[1].wait_send()
            copies[2].wait_send()

    def next_plane(value):
        lane = iota(value.shape, 1)
        return jnp.where(lane == 127, 0.0, pltpu.roll(value, 127, 1))

    def prev_plane(value):
        lane = iota(value.shape, 1)
        return jnp.where(lane == 0, 0.0, pltpu.roll(value, 1, 1))

    def cells(src, q):
        blocks = []
        for j in range(CQ):
            tail[j, 0:4, :] = corner[q, 4 * j : 4 * j + 4, :]
            tail[j, 4:5, :] = next_plane(corner[q, 4 * j : 4 * j + 1, :])
            blocks.append(
                jnp.concatenate(
                    [
                        src[q, j],
                        rim[q, j],
                        next_plane(src[q, j, pl.ds(0, 16, stride=4), :]),
                        next_plane(rim[q, j, pl.ds(0, 8, stride=4), :]),
                        tail[j],
                    ],
                    0,
                )
            )
        high, low = split(jnp.concatenate(blocks, 1))
        mapped = dot(kk[...], jnp.concatenate([high, low], 0)) + dot(klo[...], high)
        scales = srow[0:1, :]
        for j in range(CQ):
            out = mapped[:, 128 * j : 128 * j + 128] * scales
            w[q, j] = out[0:64] + maskb[...] * src[q, j]
            w[q, j, pl.ds(0, 16, stride=4), :] += prev_plane(out[96:112])
            zs[q, j] = out[64:96]
            zs[q, j, pl.ds(0, 8, stride=4), :] += prev_plane(out[112:120])
            zcs[q, 4 * j : 4 * j + 4, :] = out[120:124]
            zcs[q, 4 * j : 4 * j + 1, :] += prev_plane(out[124:125])

    def gather_rims(q):
        for j in range(CQ):
            w[q, j, 0:16, :] += zr[q, j, 0:16, :]
            for a in range(4):
                w[q, j, 16 * a : 16 * a + 4, :] += zr[q, j, 16 + 4 * a : 20 + 4 * a, :]
            w[q, j, 0:4, :] += zcr[q, 4 * j : 4 * j + 4, :]

    def operator(src, number, finish, target):
        def apply(q, carry):
            extend_arrived(src, q)
            if number > 0:
                return_sent(q)
            cells(src, q)
            return_start(q)
            return carry

        lax.fori_loop(0, NQ, apply, 0)
        return functools.partial(_finish, src, number, finish, target)

    def _finish(src, number, finish, target):
        def done(q, carry):
            return_arrived(q)
            extend_sent(src, q)
            gather_rims(q)
            finish(q)
            if number < 4:
                extend_start(target, q)
            return carry

        lax.fori_loop(0, NQ, done, 0)

    def reduce_start(stage, number, buf, value):
        start, size, pos, device = stages[stage]
        buf[start + pos] = value

        def send(i, carry):
            p = lax.rem(pos + i, size)
            here = buf.at[start + pos]
            rcopy(here, here, ss.at[number, start + p], sr.at[number, start + pos], device(p)).start()
            return carry

        lax.fori_loop(1, size, send, 0)

    def reduce_done(stage, number, buf):
        start, size, pos, device = stages[stage]

        def take(i, carry):
            p = lax.rem(pos + i, size)
            here = buf.at[start + p]
            copy = rcopy(here, here, ss.at[number, start + p], sr.at[number, start + p], device(p))
            copy.wait_recv()
            copy.wait_send()
            return carry

        lax.fori_loop(1, size, take, 0)
        total = buf[start]
        for p in range(1, size):
            total = total + buf[start + p]
        return total

    pl.semaphore_wait(
        barrier,
        2 + (n1 - 1) + (nx - 1) + (n3 - 1) + 2 * (gy > 0).astype(jnp.int32) + 2 * (gy < ny - 1).astype(jnp.int32),
    )

    def first(q, carry):
        extend_start(x0, q)
        return carry

    lax.fori_loop(0, NQ, first, 0)

    def finish0(q):
        for j in range(CQ):
            target = jnp.where(lab[...] == CQ * q + j, 1.0, 0.0)
            v[0, q, j] = target - w[q, j]

    operator(x0, 0, finish0, v.at[0])()

    stat[...] = jnp.zeros_like(stat)

    def finish1(q):
        old = v[0, q].reshape(CQ * 8, 8, 128)
        new = w[q].reshape(CQ * 8, 8, 128)
        v[1, q] = w[q]
        stat[0] += jnp.sum(old * old, 0)
        stat[1] += jnp.sum(old * new, 0)
        stat[2] += jnp.sum(new * new, 0)

    operator(v.at[0], 1, finish1, v.at[1])()

    for row in range(3):
        cs_ref[row : row + 1, :] = jnp.sum(stat[row], 0, keepdims=True)
    cs_ref[3:8, :] = jnp.zeros((5, 128), F32)
    reduce_start(0, 0, stbuf, cs_ref[...])
    rest = operator(v.at[1], 2, None, None)
    reduce_start(1, 0, stbuf, reduce_done(0, 0, stbuf))
    reduce_start(2, 0, stbuf, reduce_done(1, 0, stbuf))
    sums = jnp.sum(reduce_done(2, 0, stbuf), 1, keepdims=True)
    theta = sums[1:2] / sums[0:1]
    spread = sums[2:3] / sums[0:1] - theta * theta
    delta = 2.0 * jnp.sqrt(jnp.maximum(spread, 1e-6 * theta * theta))
    colr[0:1, :] = jnp.broadcast_to(theta, (1, 128))
    colr[1:2, :] = jnp.broadcast_to(delta, (1, 128))
    colr[2:3, :] = jnp.broadcast_to(1.0 / delta, (1, 128))

    def finish2(q):
        theta, inverse = colr[0:1, :], colr[2:3, :]
        for j in range(CQ):
            v0, u1 = v[0, q, j], v[1, q, j]
            v1 = (u1 - theta * v0) * inverse
            a1 = (w[q, j] - theta * u1) * inverse
            v[1, q, j] = v1
            v[2, q, j] = 2.0 * (a1 - theta * v1) * inverse - v0

    _finish(v.at[1], 2, finish2, v.at[2])

    def finish_next(number):
        def finish(q):
            theta, inverse = colr[0:1, :], colr[2:3, :]
            for j in range(CQ):
                v[number, q, j] = 2.0 * (w[q, j] - theta * v[number - 1, q, j]) * inverse - v[number - 2, q, j]

        return finish

    operator(v.at[2], 3, finish_next(3), v.at[3])()

    def grouped(number):
        value = v[number]
        return jnp.concatenate(
            [value[:, :, 8 * g : 8 * g + 8, :].reshape(8 * COLS, 128) for g in range(8)], 1
        )

    def grams(number, offset):
        high, low = split(grouped(number))
        yst[0:128, :] = high
        yst[128:256, :] = low

        def one(j, carry):
            high, low = split(grouped(j))
            out = dot_t(jnp.concatenate([high, low], 0), yst[...])
            out = out[0:128, 0:128] + out[0:128, 128:256] + out[128:256, 0:128] + out[128:256, 128:256]
            same = (iota((128, 128), 0) & 7) == (iota((128, 128), 1) & 7)
            out = jnp.sum(jnp.where(same, out, 0.0).reshape(COLS, 8, 128), 1)
            place = ones_where(iota((128, 128), 1) == 16 * (offset + j) + (iota((128, 128), 0) >> 3))
            gres[...] += exact_dot(out, place)
            return carry

        lax.fori_loop(0, 4, one, 0)

    gres[...] = jnp.zeros_like(gres)
    grams(0, 0)
    operator(v.at[3], 4, finish_next(4), None)()
    grams(4, 4)

    reduce_start(0, 1, gbuf, gres[...])
    reduce_start(1, 1, gbuf, reduce_done(0, 1, gbuf))
    reduce_start(2, 1, gbuf, reduce_done(1, 1, gbuf))
    blocks = reduce_done(2, 1, gbuf)

    theta, delta = colr[0:1, :], colr[1:2, :]
    parts = exact_dot(blocks, table[...])
    for i in range(4):
        at = [parts[:, 128 * (4 * which + i) : 128 * (4 * which + i) + 128] for which in range(3)]
        gm[16 * i : 16 * i + 16, :] = theta * at[0] + delta * at[1] + at[2]

    def eliminate(k, carry):
        row = gm[pl.ds(k, 1), :]
        value = gm[...]
        here = iota((64, 128), 1) == k
        col = jnp.sum(jnp.where(here, value, 0.0), 1, keepdims=True)
        pivot = jnp.sum(jnp.where(iota((1, 128), 1) == k, row, 0.0), 1, keepdims=True)
        row = row / pivot
        gm[...] = jnp.where(iota((64, 128), 0) == k, row, value - col * row)
        return carry

    lax.fori_loop(0, 64, eliminate, 0)

    c = [gm[16 * j : 16 * j + 16, :] for j in range(4)]
    half = 0.5 * delta
    unit = jnp.where(iota((16, 128), 0) == iota((16, 128), 1) - 64, 1.0, 0.0)
    e = [
        unit - theta * c[0] - half * c[1],
        -(theta * c[1] + delta * c[0] + half * c[2]),
        -(theta * c[2] + half * (c[1] + c[3])),
        -(theta * c[3] + half * c[2]),
        -(half * c[3]),
    ]
    nothing = jnp.zeros((16, 128), F32)
    forx = jnp.concatenate(c + [nothing] * 4, 0).T
    forr = jnp.concatenate(e + [nothing] * 3, 0).T
    coef = jnp.concatenate([forx[64:80], forr[64:80]], 0)
    spread_in = ones_where((iota((128, 640), 1) >> 3) == iota((128, 640), 0))
    spread_out = ones_where((iota((256, 32), 0) >> 3) == iota((256, 32), 1))
    same = (iota((256, 640), 0) & 7) == (iota((256, 640), 1) & 7)

    def wide(value):
        value = dot(spread_out, dot(value, spread_in).astype(BF))
        return jnp.where(same, value, 0.0).astype(BF)

    chigh, clow = split(coef)
    chigh, clow = wide(chigh), wide(clow)
    for g in range(8):
        field = jnp.concatenate(
            [v[j, :, :, 8 * g : 8 * g + 8, :].reshape(8 * COLS, 128) for j in range(5)], 0
        )
        high, low = split(field)
        out = dot(chigh, high) + dot(chigh, low) + dot(clow, high)
        xo[:, :, 8 * g : 8 * g + 8, :] = x0[:, :, 8 * g : 8 * g + 8, :] + out[0:128].reshape(NQ, CQ, 8, 128)
        ro[:, :, 8 * g : 8 * g + 8, :] = out[128:256].reshape(NQ, CQ, 8, 128)

    for q in range(NQ):
        return_sent(q)


def on_device(start_block, labels, materials, mat_scales, cell_stiffness):
    nx, ny = lax.axis_size("gx"), lax.axis_size("gy")
    n1 = 8 if ny % 8 == 0 else 2
    slots = n1 + nx + ny // n1
    vmem = pl.BlockSpec(memory_space=pltpu.VMEM)
    block = jax.ShapeDtypeStruct((NQ, CQ, 64, 128), F32)
    out = pl.pallas_call(
        functools.partial(kernel, nx, ny, n1),
        out_shape=(block, block),
        in_specs=[vmem, vmem, vmem, pl.BlockSpec(memory_space=pltpu.SMEM), vmem, vmem, vmem],
        out_specs=(vmem, vmem),
        scratch_shapes=[
            pltpu.VMEM((5, NQ, CQ, 64, 128), F32),
            pltpu.VMEM((NQ, CQ, 64, 128), F32),
            pltpu.VMEM((NQ, CQ, 32, 128), F32),
            pltpu.VMEM((NQ, 4 * CQ, 128), F32),
            pltpu.VMEM((NQ, CQ, 16, 128), F32),
            pltpu.VMEM((NQ, 4 * CQ, 128), F32),
            pltpu.VMEM((NQ, CQ, 32, 128), F32),
            pltpu.VMEM((NQ, 4 * CQ, 128), F32),
            pltpu.VMEM((NQ, CQ, 32, 128), F32),
            pltpu.VMEM((NQ, 4 * CQ, 128), F32),
            pltpu.VMEM((CQ, 8, 128), F32),
            pltpu.VMEM((128, 128), F32),
            pltpu.VMEM((128, 256), BF),
            pltpu.VMEM((128, 128), BF),
            pltpu.VMEM((64, 128), F32),
            pltpu.VMEM((8, 128), F32),
            pltpu.VMEM((3, 8, 128), F32),
            pltpu.VMEM((slots, 8, 128), F32),
            pltpu.VMEM((slots, 16, 128), F32),
            pltpu.VMEM((64, 128), F32),
            pltpu.VMEM((256, 1024), BF),
            pltpu.VMEM((16, 128), F32),
            pltpu.VMEM((8, 128), F32),
            pltpu.VMEM((8, 128), F32),
            pltpu.SemaphoreType.DMA((3, NQ)),
            pltpu.SemaphoreType.DMA((3, NQ)),
            pltpu.SemaphoreType.DMA((3, NQ)),
            pltpu.SemaphoreType.DMA((3, NQ)),
            pltpu.SemaphoreType.DMA((2, slots)),
            pltpu.SemaphoreType.DMA((2, slots)),
        ],
        compiler_params=pltpu.CompilerParams(
            collective_id=0, has_side_effects=True, vmem_limit_bytes=48 * 1024 * 1024
        ),
    )(
        start_block.reshape(NQ, CQ, 64, 128),
        labels.reshape(64, 128),
        materials.reshape(1, 128),
        mat_scales,
        cell_stiffness,
        jnp.asarray(order_matrix()),
        jnp.asarray(moment_tables()),
    )
    return tuple(one.reshape(start_block.shape) for one in out)


def solution(mesh):
    spread = P(None, "gx", "gy", None, None)
    return jax.shard_map(
        on_device,
        mesh=mesh,
        in_specs=(spread, P("gx", "gy", None, None), P("gx", "gy", None), P(), P()),
        out_specs=(spread, spread),
        check_vma=False,
    )
```

time: 1210 us -> 130 us (0.11); the launches traced: 1190 us -> 129 us
  blocking collectives: 699 us -> 0 us
  local copies, waits for them, and re-layouts: 284 us -> 6.63 us
  Pallas kernels: 0 us -> 121 us
  starting transfers between devices: 58.7 us -> 0 us
  other arithmetic: 57.8 us -> 0 us
  waiting for transfers between devices: 57 us -> 0 us
  matrix products: 32.1 us -> 0 us
    psum x7 -> x0, blocking collectives: 699 us -> none  [the longest x3 301 us: on_device(): curv = lax.psum(gram(direction, image), ('gx', 'gy'))]
    concatenate x151 -> x0, local copies, waits for them, and re-layouts: 251 us -> none  [the longest x5 114 us: assemble(): return jnp.concatenate(slabs, 3)]
    pallas_call x0 -> x1, Pallas kernels: none -> 121 us  [on_device(): pl.pallas_call(functools.partial(kernel, nx, ny, n1), out_shape=(block, b...]
    ppermute x20 -> x0, starting transfers between devices: 58.7 us -> none  [the longest x10 33 us: passed_along(): return lax.ppermute(value, axis, pairs)]
    ppermute x20 -> x0, waiting for transfers between devices: 57 us -> none  [the longest x10 44.1 us: passed_along(): return lax.ppermute(value, axis, pairs)]
    dot_general x24 -> x0, matrix products: 29.3 us -> none  [the longest x11 11 us: combine(): jnp.dot(coef.T, block.reshape(columns, -1), precision=lax.Precision.HIGHEST)]
    another operation x37 -> x0, other arithmetic: 29.1 us -> none  [the longest x21 15 us: solve_spd(): factor = jnp.linalg.cholesky(matrix)]
    slice x66 -> x0, local copies, waits for them, and re-layouts: 24.1 us -> none  [the longest x15 5.22 us: next_plane(): values[..., 1:]]
  transfers between devices with their start and end apart: 20 -> 0, of which waited for: 14 -> 0; matrix products, arithmetic and copies ran while one was open for 7% -> 0% of each run, Pallas kernels for 0% -> 0%
where the time goes in v1:
time: 130 us; the launch traced here: 129 us
  Pallas kernels  121 us (93%)
  local copies, waits for them, and re-layouts  6.63 us (5%)
    pallas_call x1, Pallas kernels, on_device(): pl.pallas_call(functools.partial(kernel, nx, ny, n1), out_shape=(block, b...  121 us
    unnamed x16, local copies, waits for them, and re-layouts  6.63 us

profile of v1, /device:TPU:1, one launch (start us, length us, event | category | flops | bytes accessed | tf_op | source)
XLA Modules:
  0.0 128.7 jit_solution(17448059252275062154)
XLA Ops:
  0.6 0.0 copy-start.5
  0.6 0.0 copy-start.6
  0.7 0.6 copy-done.5
  1.3 0.0 copy-done.6
  1.3 0.0 copy-start
  1.3 1.0 copy-done
  2.3 0.0 copy-start.1
  2.3 1.0 copy-done.1
  3.3 0.0 copy-start.2
  3.3 0.8 copy-done.2
  4.2 0.0 copy-start.3
  4.2 0.8 copy-done.3
  4.9 0.0 copy-start.4
  4.9 0.8 copy-done.4
  5.7 121.4 %shard_map.86 = (f32[4,4,64,128]{3,2,1,0:T(8,128)S(1)}, f32[4,4,64,128]{3,2,1,0:T(8,128)S(1)}) custom-call(f32[4,4,64,128]{3,2,1,0:T(8,128)S(1)} %bitcast.9, s32[64,128]{1,0:T(8,128)S(1)} %bitcast.12, s32[1,128]{1,0:T(1,128)S(1)} %bitcast.13, f32[8]{0:T(128)S(1)} %copy-done.6, f32[125,125]{1,0:T(8,128)S(1)} %copy-done.2, bf16[128,128]{1,0:T(8,128)(2,1)S(1)} %copy-done.4, ...), custom_call_target="tpu_custom_call" | custom-call | tf_op jit(solution)/shard_map/pallas_call | solution.py:513
  127.1 0.8 copy.13
  127.9 0.8 copy.14
Async XLA Ops:
  0.6 0.7 copy-start.5
  0.6 0.7 copy-start.6
  1.3 1.0 copy-start
  2.3 1.0 copy-start.1
  3.3 0.8 copy-start.2
  4.2 0.8 copy-start.3
  4.9 0.8 copy-start.4

commit v2 on v1

--- a/solution.py
+++ b/solution.py
@@ -37,13 +37,13 @@
 
 
 def moment_tables():
-    mu = np.zeros((8, 8))
-    for k in range(4):
-        mu[k, k] = 1.0
-    mu[4, 4] = 1.0
+    mu = np.zeros((7, 8))
+    for k in range(3):
+        mu[k, 4 + k] = 1.0
+    mu[3, 0] = 1.0
     for i in (1, 2, 3):
-        mu[4 + i, 4 + i] = 2.0
-        mu[4 + i] -= mu[4 - i]
+        mu[3 + i, i] = 2.0
+        mu[3 + i] -= mu[3 - i]
 
     def inner(i, j):
         return 0.5 * (mu[i + j] + mu[abs(i - j)])
@@ -51,8 +51,9 @@
     tables = np.zeros((3, 4, 8, 8))
     for i in range(4):
         for j in range(4):
-            tables[0, i, :, j] = inner(i, j)
-            tables[1, i, :, j] = 0.5 * (inner(i, j + 1) + inner(i, abs(j - 1)))
+            if i + j < 6:
+                tables[0, i, :, j] = inner(i, j)
+                tables[1, i, :, j] = 0.5 * (inner(i, j + 1) + inner(i, abs(j - 1)))
         tables[2, i, :, 4] = inner(i, 0)
     out = np.zeros((128, 3 * 4 * 128), np.float32)
     for which in range(3):
@@ -95,16 +96,25 @@
 
 
 def kernel(
-    nx, ny, n1,
+    nx, ny,
+    x0_in, lab_in, mat_in, ms_in, kin_in, order_in, table_in,
+    xo, ro,
     x0, lab, mat, ms, kin, order, table,
-    xo, ro,
-    v, w, rim, corner, ysend, csend, zs, zcs, zr, zcr, tail, kpad, kk, klo, maskb, srow,
-    stat, stbuf, gbuf, gm, yst, gres, colr, cs_ref,
-    es, er, rs, rr, ss, sr,
+    v, w, rim, corner, ysend, csend, zs, zcs, zr, zcr, tail, zct, kpad, kk, klo, maskb, srow,
+    gbuf, fbuf, gm, yst, gres, colr, fhigh, flow,
+    es, er, rs, rr, ss, sr, ins,
 ):
+    fetches = [
+        pltpu.make_async_copy(src, dst, ins.at[n])
+        for n, (src, dst) in enumerate(
+            ((x0_in, x0), (kin_in, kin), (order_in, order), (ms_in, ms), (lab_in, lab), (mat_in, mat), (table_in, table))
+        )
+    ]
+    for fetch in fetches:
+        fetch.start()
+
     gx = lax.axis_index("gx")
     gy = lax.axis_index("gy")
-    n3 = ny // n1
     xprev = lax.rem(gx + nx - 1, nx)
     xnext = lax.rem(gx + 1, nx)
     has_prev = gy > 0
@@ -112,12 +122,16 @@
     yprev = lax.max(gy - 1, 0)
     ynext = lax.min(gy + 1, ny - 1)
 
-    pos1 = lax.rem(gy, n1)
-    pos3 = lax.div(gy, n1)
+    half = ny // 2
+    nz = half // 2
+    nxx = nx // 4
+    y_lo, x_hi = lax.rem(gx, 4), lax.div(gx, 4)
+    y_hi, in_half = lax.div(gy, half), lax.rem(gy, half)
+    z, core = lax.div(in_half, 2), lax.rem(in_half, 2)
     stages = (
-        (0, n1, pos1, lambda p: (gx, gy - pos1 + p)),
-        (n1, nx, gx, lambda p: (p, gy)),
-        (n1 + nx, n3, pos3, lambda p: (gx, p * n1 + pos1)),
+        (0, 8, 4 * y_hi + y_lo, lambda p: (4 * x_hi + lax.rem(p, 4), half * lax.div(p, 4) + in_half)),
+        (8, nz, z, lambda p: (gx, half * y_hi + 2 * p + core)),
+        (8 + nz, 2 * nxx, 2 * x_hi + core, lambda p: (4 * lax.div(p, 2) + y_lo, half * y_hi + 2 * z + lax.rem(p, 2))),
     )
 
     barrier = pltpu.get_barrier_semaphore()
@@ -146,6 +160,10 @@
         lax.fori_loop(1, size, hello, 0)
 
     kpad[...] = jnp.zeros_like(kpad)
+    zct[...] = jnp.zeros_like(zct)
+    tail[...] = jnp.zeros_like(tail)
+    for fetch in fetches:
+        fetch.wait()
     kpad[0:125, 0:125] = kin[...]
     khigh, klow = split(kpad[...])
     pm = order[...]
@@ -159,10 +177,24 @@
     klo[...] = permuted(klow)
     maskb[...] = jnp.where(lab[...] >= 0, PENALTY, 0.0)
     scale = jnp.zeros((1, 128), F32)
+    largest = jnp.zeros((1, 128), F32)
     for which in range(8):
         scale = scale + jnp.where(mat[...] == which, ms[which], 0.0)
+        largest = jnp.maximum(largest, jnp.full((1, 128), ms[which], F32))
     srow[...] = jnp.broadcast_to(scale, (8, 128))
-    tail[...] = jnp.zeros_like(tail)
+
+    def total(value):
+        return jnp.sum(jnp.sum(value, 0, keepdims=True), 1, keepdims=True)
+
+    size = jnp.sqrt(jnp.maximum(total(kpad[...] * kpad[...]), 1e-30))
+    unit_k = (kpad[...] / size).astype(BF)
+    squared = dot(unit_k, unit_k).astype(BF)
+    fourth = dot(squared, squared)
+    top = size * jnp.sqrt(jnp.sqrt(jnp.sqrt(total(fourth * fourth))))
+    top = PENALTY + largest * top
+    colr[0:1, :] = 0.6 * top
+    colr[1:2, :] = 0.35 * top
+    colr[2:3, :] = 1.0 / (0.35 * top)
 
     @pl.when(jnp.logical_not(has_next))
     def _():
@@ -264,8 +296,8 @@
     def cells(src, q):
         blocks = []
         for j in range(CQ):
-            tail[j, 0:4, :] = corner[q, 4 * j : 4 * j + 4, :]
-            tail[j, 4:5, :] = next_plane(corner[q, 4 * j : 4 * j + 1, :])
+            tail[q, j, 0:4, :] = corner[q, 4 * j : 4 * j + 4, :]
+            tail[q, j, 4:5, :] = next_plane(corner[q, 4 * j : 4 * j + 1, :])
             blocks.append(
                 jnp.concatenate(
                     [
@@ -273,7 +305,7 @@
                         rim[q, j],
                         next_plane(src[q, j, pl.ds(0, 16, stride=4), :]),
                         next_plane(rim[q, j, pl.ds(0, 8, stride=4), :]),
-                        tail[j],
+                        tail[q, j],
                     ],
                     0,
                 )
@@ -287,8 +319,9 @@
             w[q, j, pl.ds(0, 16, stride=4), :] += prev_plane(out[96:112])
             zs[q, j] = out[64:96]
             zs[q, j, pl.ds(0, 8, stride=4), :] += prev_plane(out[112:120])
-            zcs[q, 4 * j : 4 * j + 4, :] = out[120:124]
-            zcs[q, 4 * j : 4 * j + 1, :] += prev_plane(out[124:125])
+            zct[q, j, 0:4, :] = out[120:124]
+            zct[q, j, 0:1, :] += prev_plane(out[124:125])
+            zcs[q, 4 * j : 4 * j + 4, :] = zct[q, j, 0:4, :]
 
     def gather_rims(q):
         for j in range(CQ):
@@ -352,7 +385,7 @@
 
     pl.semaphore_wait(
         barrier,
-        2 + (n1 - 1) + (nx - 1) + (n3 - 1) + 2 * (gy > 0).astype(jnp.int32) + 2 * (gy < ny - 1).astype(jnp.int32),
+        2 + 7 + (nz - 1) + (2 * nxx - 1) + 2 * (gy > 0).astype(jnp.int32) + 2 * (gy < ny - 1).astype(jnp.int32),
     )
 
     def first(q, carry):
@@ -368,43 +401,12 @@
 
     operator(x0, 0, finish0, v.at[0])()
 
-    stat[...] = jnp.zeros_like(stat)
-
     def finish1(q):
-        old = v[0, q].reshape(CQ * 8, 8, 128)
-        new = w[q].reshape(CQ * 8, 8, 128)
-        v[1, q] = w[q]
-        stat[0] += jnp.sum(old * old, 0)
-        stat[1] += jnp.sum(old * new, 0)
-        stat[2] += jnp.sum(new * new, 0)
-
-    operator(v.at[0], 1, finish1, v.at[1])()
-
-    for row in range(3):
-        cs_ref[row : row + 1, :] = jnp.sum(stat[row], 0, keepdims=True)
-    cs_ref[3:8, :] = jnp.zeros((5, 128), F32)
-    reduce_start(0, 0, stbuf, cs_ref[...])
-    rest = operator(v.at[1], 2, None, None)
-    reduce_start(1, 0, stbuf, reduce_done(0, 0, stbuf))
-    reduce_start(2, 0, stbuf, reduce_done(1, 0, stbuf))
-    sums = jnp.sum(reduce_done(2, 0, stbuf), 1, keepdims=True)
-    theta = sums[1:2] / sums[0:1]
-    spread = sums[2:3] / sums[0:1] - theta * theta
-    delta = 2.0 * jnp.sqrt(jnp.maximum(spread, 1e-6 * theta * theta))
-    colr[0:1, :] = jnp.broadcast_to(theta, (1, 128))
-    colr[1:2, :] = jnp.broadcast_to(delta, (1, 128))
-    colr[2:3, :] = jnp.broadcast_to(1.0 / delta, (1, 128))
-
-    def finish2(q):
         theta, inverse = colr[0:1, :], colr[2:3, :]
         for j in range(CQ):
-            v0, u1 = v[0, q, j], v[1, q, j]
-            v1 = (u1 - theta * v0) * inverse
-            a1 = (w[q, j] - theta * u1) * inverse
-            v[1, q, j] = v1
-            v[2, q, j] = 2.0 * (a1 - theta * v1) * inverse - v0
-
-    _finish(v.at[1], 2, finish2, v.at[2])
+            v[1, q, j] = (w[q, j] - theta * v[0, q, j]) * inverse
+
+    operator(v.at[0], 1, finish1, v.at[1])()
 
     def finish_next(number):
         def finish(q):
@@ -414,43 +416,60 @@
 
         return finish
 
+    operator(v.at[1], 2, finish_next(2), v.at[2])()
+
+    def grouped(value):
+        return [
+            value[:, :, 8 * g : 8 * g + 8, :].reshape(8 * COLS, 128) for g in range(value.shape[2] // 8)
+        ]
+
+    def stacked(groups):
+        high, low = split(jnp.concatenate(groups, 1))
+        return jnp.concatenate([high, low], 0)
+
+    def block(left, right):
+        out = dot_t(left, right)
+        out = out[0:128, 0:128] + out[0:128, 128:256] + out[128:256, 0:128] + out[128:256, 128:256]
+        same = (iota((128, 128), 0) & 7) == (iota((128, 128), 1) & 7)
+        return jnp.sum(jnp.where(same, out, 0.0).reshape(COLS, 8, 128), 1)
+
+    def placed(value, lane):
+        return exact_dot(value, ones_where(iota((128, 128), 1) == lane + (iota((128, 128), 0) >> 3)))
+
+    def grams(number, count, offset):
+        yst[...] = stacked(grouped(v[number]))
+
+        def one(j, carry):
+            gres[...] += placed(block(stacked(grouped(v[j])), yst[...]), 16 * (offset + j))
+            return carry
+
+        lax.fori_loop(0, count, one, 0)
+
+    gres[...] = jnp.zeros_like(gres)
+    grams(0, 3, 4)
     operator(v.at[2], 3, finish_next(3), v.at[3])()
-
-    def grouped(number):
-        value = v[number]
-        return jnp.concatenate(
-            [value[:, :, 8 * g : 8 * g + 8, :].reshape(8 * COLS, 128) for g in range(8)], 1
-        )
-
-    def grams(number, offset):
-        high, low = split(grouped(number))
-        yst[0:128, :] = high
-        yst[128:256, :] = low
-
-        def one(j, carry):
-            high, low = split(grouped(j))
-            out = dot_t(jnp.concatenate([high, low], 0), yst[...])
-            out = out[0:128, 0:128] + out[0:128, 128:256] + out[128:256, 0:128] + out[128:256, 128:256]
-            same = (iota((128, 128), 0) & 7) == (iota((128, 128), 1) & 7)
-            out = jnp.sum(jnp.where(same, out, 0.0).reshape(COLS, 8, 128), 1)
-            place = ones_where(iota((128, 128), 1) == 16 * (offset + j) + (iota((128, 128), 0) >> 3))
-            gres[...] += exact_dot(out, place)
-            return carry
-
-        lax.fori_loop(0, 4, one, 0)
-
-    gres[...] = jnp.zeros_like(gres)
-    grams(0, 0)
-    operator(v.at[3], 4, finish_next(4), None)()
-    grams(4, 4)
-
-    reduce_start(0, 1, gbuf, gres[...])
-    reduce_start(1, 1, gbuf, reduce_done(0, 1, gbuf))
-    reduce_start(2, 1, gbuf, reduce_done(1, 1, gbuf))
-    blocks = reduce_done(2, 1, gbuf)
+    grams(3, 4, 0)
+    reduce_start(0, 0, gbuf, gres[...])
+    rest = operator(v.at[3], 4, finish_next(4), None)
+
+    last = block(
+        stacked(grouped(v[3]) + grouped(rim[...]) + grouped(tail[...])),
+        stacked(grouped(w[...]) + grouped(zs[...]) + grouped(zct[...])),
+    )
+    last = placed(last[0:8], 48) + placed(last[8:16], 64)
+    reduce_start(0, 1, fbuf, last)
+    reduce_start(1, 0, gbuf, reduce_done(0, 0, gbuf))
+    rest()
+    reduce_start(1, 1, fbuf, reduce_done(0, 1, fbuf))
+    reduce_start(2, 0, gbuf, reduce_done(1, 0, gbuf))
+    for j in range(5):
+        high, low = split(jnp.concatenate(grouped(v[j]), 1))
+        fhigh[128 * j : 128 * j + 128, :] = high
+        flow[128 * j : 128 * j + 128, :] = low
+    reduce_start(2, 1, fbuf, reduce_done(1, 1, fbuf))
 
     theta, delta = colr[0:1, :], colr[1:2, :]
-    parts = exact_dot(blocks, table[...])
+    parts = exact_dot(reduce_done(2, 0, gbuf), table[...])
     for i in range(4):
         at = [parts[:, 128 * (4 * which + i) : 128 * (4 * which + i) + 128] for which in range(3)]
         gm[16 * i : 16 * i + 16, :] = theta * at[0] + delta * at[1] + at[2]
@@ -465,7 +484,12 @@
         gm[...] = jnp.where(iota((64, 128), 0) == k, row, value - col * row)
         return carry
 
-    lax.fori_loop(0, 64, eliminate, 0)
+    lax.fori_loop(0, 48, eliminate, 0)
+    last = reduce_done(2, 1, fbuf)
+    inside = (iota((8, 128), 1) >= 48) & (iota((8, 128), 1) < 64)
+    gm[48:56, :] += jnp.where(inside, last, 0.0)
+    gm[56:64, :] += jnp.where(inside, pltpu.roll(last, 112, 1), 0.0)
+    lax.fori_loop(48, 64, eliminate, 0)
 
     c = [gm[16 * j : 16 * j + 16, :] for j in range(4)]
     half = 0.5 * delta
@@ -491,14 +515,14 @@
 
     chigh, clow = split(coef)
     chigh, clow = wide(chigh), wide(clow)
-    for g in range(8):
-        field = jnp.concatenate(
-            [v[j, :, :, 8 * g : 8 * g + 8, :].reshape(8 * COLS, 128) for j in range(5)], 0
-        )
-        high, low = split(field)
+    for pair in range(4):
+        at = slice(256 * pair, 256 * pair + 256)
+        high, low = fhigh[:, at], flow[:, at]
         out = dot(chigh, high) + dot(chigh, low) + dot(clow, high)
-        xo[:, :, 8 * g : 8 * g + 8, :] = x0[:, :, 8 * g : 8 * g + 8, :] + out[0:128].reshape(NQ, CQ, 8, 128)
-        ro[:, :, 8 * g : 8 * g + 8, :] = out[128:256].reshape(NQ, CQ, 8, 128)
+        for g in (2 * pair, 2 * pair + 1):
+            one = out[:, 128 * (g - 2 * pair) : 128 * (g - 2 * pair) + 128]
+            xo[:, :, 8 * g : 8 * g + 8, :] = x0[:, :, 8 * g : 8 * g + 8, :] + one[0:128].reshape(NQ, CQ, 8, 128)
+            ro[:, :, 8 * g : 8 * g + 8, :] = one[128:256].reshape(NQ, CQ, 8, 128)
 
     for q in range(NQ):
         return_sent(q)
@@ -506,16 +530,22 @@
 
 def on_device(start_block, labels, materials, mat_scales, cell_stiffness):
     nx, ny = lax.axis_size("gx"), lax.axis_size("gy")
-    n1 = 8 if ny % 8 == 0 else 2
-    slots = n1 + nx + ny // n1
+    slots = 8 + ny // 4 + nx // 2
     vmem = pl.BlockSpec(memory_space=pltpu.VMEM)
     block = jax.ShapeDtypeStruct((NQ, CQ, 64, 128), F32)
     out = pl.pallas_call(
-        functools.partial(kernel, nx, ny, n1),
+        functools.partial(kernel, nx, ny),
         out_shape=(block, block),
-        in_specs=[vmem, vmem, vmem, pl.BlockSpec(memory_space=pltpu.SMEM), vmem, vmem, vmem],
+        in_specs=[pl.BlockSpec(memory_space=pltpu.HBM)] * 7,
         out_specs=(vmem, vmem),
         scratch_shapes=[
+            pltpu.VMEM((NQ, CQ, 64, 128), F32),
+            pltpu.VMEM((64, 128), jnp.int32),
+            pltpu.VMEM((1, 128), jnp.int32),
+            pltpu.SMEM((8,), F32),
+            pltpu.VMEM((125, 125), F32),
+            pltpu.VMEM((128, 128), BF),
+            pltpu.VMEM((128, 1536), BF),
             pltpu.VMEM((5, NQ, CQ, 64, 128), F32),
             pltpu.VMEM((NQ, CQ, 64, 128), F32),
             pltpu.VMEM((NQ, CQ, 32, 128), F32),
@@ -526,29 +556,31 @@
             pltpu.VMEM((NQ, 4 * CQ, 128), F32),
             pltpu.VMEM((NQ, CQ, 32, 128), F32),
             pltpu.VMEM((NQ, 4 * CQ, 128), F32),
-            pltpu.VMEM((CQ, 8, 128), F32),
+            pltpu.VMEM((NQ, CQ, 8, 128), F32),
+            pltpu.VMEM((NQ, CQ, 8, 128), F32),
             pltpu.VMEM((128, 128), F32),
             pltpu.VMEM((128, 256), BF),
             pltpu.VMEM((128, 128), BF),
             pltpu.VMEM((64, 128), F32),
             pltpu.VMEM((8, 128), F32),
-            pltpu.VMEM((3, 8, 128), F32),
+            pltpu.VMEM((slots, 16, 128), F32),
             pltpu.VMEM((slots, 8, 128), F32),
-            pltpu.VMEM((slots, 16, 128), F32),
             pltpu.VMEM((64, 128), F32),
             pltpu.VMEM((256, 1024), BF),
             pltpu.VMEM((16, 128), F32),
             pltpu.VMEM((8, 128), F32),
-            pltpu.VMEM((8, 128), F32),
+            pltpu.VMEM((640, 1024), BF),
+            pltpu.VMEM((640, 1024), BF),
             pltpu.SemaphoreType.DMA((3, NQ)),
             pltpu.SemaphoreType.DMA((3, NQ)),
             pltpu.SemaphoreType.DMA((3, NQ)),
             pltpu.SemaphoreType.DMA((3, NQ)),
             pltpu.SemaphoreType.DMA((2, slots)),
             pltpu.SemaphoreType.DMA((2, slots)),
+            pltpu.SemaphoreType.DMA((7,)),
         ],
         compiler_params=pltpu.CompilerParams(
-            collective_id=0, has_side_effects=True, vmem_limit_bytes=48 * 1024 * 1024
+            collective_id=0, has_side_effects=True, vmem_limit_bytes=56 * 1024 * 1024
         ),
     )(
         start_block.reshape(NQ, CQ, 64, 128),

time: 130 us -> 111 us (0.85)
  Pallas kernels: 121 us -> 107 us
  local copies, waits for them, and re-layouts: 6.63 us -> 2.74 us
    pallas_call x1, Pallas kernels: 121 us -> 107 us  [on_device(): pl.pallas_call(functools.partial(kernel, nx, ny), out_shape=(block, block...]
    unnamed x16 -> x4, local copies, waits for them, and re-layouts: 6.63 us -> 2.74 us
where the time goes in v2:
time: 111 us; the launch traced here: 110 us
  Pallas kernels  107 us (96%)
  local copies, waits for them, and re-layouts  2.74 us (2%)
    pallas_call x1, Pallas kernels, on_device(): pl.pallas_call(functools.partial(kernel, nx, ny), out_shape=(block, block...  107 us
    unnamed x4, local copies, waits for them, and re-layouts  2.74 us

profile of v2, /device:TPU:1, one launch (start us, length us, event | category | flops | bytes accessed | tf_op | source)
XLA Modules:
  0.0 110.3 jit_solution(12194665314661570755)
XLA Ops:
  0.6 106.9 %shard_map.86 = (f32[4,4,64,128]{3,2,1,0:T(8,128)}, f32[4,4,64,128]{3,2,1,0:T(8,128)}) custom-call(f32[4,4,64,128]{3,2,1,0:T(8,128)} %bitcast.9, s32[64,128]{1,0:T(8,128)} %bitcast.12, s32[1,128]{1,0:T(1,128)} %bitcast.13, f32[8]{0:T(128)} %ms_in.1, f32[125,125]{1,0:T(8,128)} %kin_in.1, bf16[128,128]{1,0:T(8,128)(2,1)} %constant.4.clone.order_in, ...), custom_call_target="tpu_custom_call" | custom-call | tf_op jit(solution)/shard_map/pallas_call | solution.py:536
  107.6 0.0 copy-start
  107.6 1.9 %copy.13 = f32[16,1,1,64,128]{4,3,2,1,0:T(8,128)} copy(f32[16,1,1,64,128]{4,3,2,1,0:T(8,128)} %bitcast.11) | data formatting | bytes 1048576
  109.5 0.0 copy-done
  109.5 0.8 copy.14
Async XLA Ops:
  107.6 2.0 %copy-start = (f32[4,4,64,128]{3,2,1,0:T(8,128)S(1)}, f32[4,4,64,128]{3,2,1,0:T(8,128)}, u32[]{:S(2)}) copy-start(f32[4,4,64,128]{3,2,1,0:T(8,128)} %get-tuple-element.5) | copy-start | bytes 1572868

commit v3 on v2

--- a/solution.py
+++ b/solution.py
@@ -10,7 +10,7 @@
 from jax.sharding import PartitionSpec as P
 
 COLS = 16
-NQ = 4
+NQ = 8
 CQ = COLS // NQ
 PENALTY = 1.0
 MESH = pl.DeviceIdType.MESH
@@ -129,9 +129,9 @@
     y_hi, in_half = lax.div(gy, half), lax.rem(gy, half)
     z, core = lax.div(in_half, 2), lax.rem(in_half, 2)
     stages = (
-        (0, 8, 4 * y_hi + y_lo, lambda p: (4 * x_hi + lax.rem(p, 4), half * lax.div(p, 4) + in_half)),
-        (8, nz, z, lambda p: (gx, half * y_hi + 2 * p + core)),
-        (8 + nz, 2 * nxx, 2 * x_hi + core, lambda p: (4 * lax.div(p, 2) + y_lo, half * y_hi + 2 * z + lax.rem(p, 2))),
+        (0, 2 * nxx, 2 * x_hi + core, lambda p: (4 * lax.div(p, 2) + y_lo, half * y_hi + 2 * z + lax.rem(p, 2))),
+        (2 * nxx, nz, z, lambda p: (gx, half * y_hi + 2 * p + core)),
+        (2 * nxx + nz, 8, 4 * y_hi + y_lo, lambda p: (4 * x_hi + lax.rem(p, 4), half * lax.div(p, 4) + in_half)),
     )
 
     barrier = pltpu.get_barrier_semaphore()
@@ -233,12 +233,13 @@
                 ysend[q, j, 4 * a : 4 * a + 4, :] = src[q, j, 16 * a : 16 * a + 4, :]
             csend[q, 4 * j : 4 * j + 4, :] = src[q, j, 0:4, :]
         copies = ext(src, q)
-        copies[0].start()
 
         @pl.when(has_prev)
         def _():
+            copies[2].start()
             copies[1].start()
-            copies[2].start()
+
+        copies[0].start()
 
     def extend_arrived(src, q):
         copies = ext(src, q)
@@ -260,12 +261,13 @@
 
     def return_start(q):
         copies = ret(q)
-        copies[0].start()
 
         @pl.when(has_next)
         def _():
+            copies[2].start()
             copies[1].start()
-            copies[2].start()
+
+        copies[0].start()
 
     def return_arrived(q):
         copies = ret(q)
@@ -342,6 +344,40 @@
         lax.fori_loop(0, NQ, apply, 0)
         return functools.partial(_finish, src, number, finish, target)
 
+    def operate(src, number, finish, target):
+        lag = NQ - 2
+
+        def apply(q):
+            extend_arrived(src, q)
+            if number > 0:
+                return_sent(q)
+            cells(src, q)
+            return_start(q)
+
+        def done(q):
+            return_arrived(q)
+            extend_sent(src, q)
+            gather_rims(q)
+            finish(q)
+            extend_start(target, q)
+
+        def lead(q, carry):
+            apply(q)
+            return carry
+
+        def both(q, carry):
+            apply(q)
+            done(q - lag)
+            return carry
+
+        def trail(q, carry):
+            done(q)
+            return carry
+
+        lax.fori_loop(0, lag, lead, 0)
+        lax.fori_loop(lag, NQ, both, 0)
+        lax.fori_loop(NQ - lag, NQ, trail, 0)
+
     def _finish(src, number, finish, target):
         def done(q, carry):
             return_arrived(q)
@@ -399,14 +435,14 @@
             target = jnp.where(lab[...] == CQ * q + j, 1.0, 0.0)
             v[0, q, j] = target - w[q, j]
 
-    operator(x0, 0, finish0, v.at[0])()
+    operate(x0, 0, finish0, v.at[0])
 
     def finish1(q):
         theta, inverse = colr[0:1, :], colr[2:3, :]
         for j in range(CQ):
             v[1, q, j] = (w[q, j] - theta * v[0, q, j]) * inverse
 
-    operator(v.at[0], 1, finish1, v.at[1])()
+    operate(v.at[0], 1, finish1, v.at[1])
 
     def finish_next(number):
         def finish(q):
@@ -416,7 +452,7 @@
 
         return finish
 
-    operator(v.at[1], 2, finish_next(2), v.at[2])()
+    operate(v.at[1], 2, finish_next(2), v.at[2])
 
     def grouped(value):
         return [
@@ -447,7 +483,7 @@
 
     gres[...] = jnp.zeros_like(gres)
     grams(0, 3, 4)
-    operator(v.at[2], 3, finish_next(3), v.at[3])()
+    operate(v.at[2], 3, finish_next(3), v.at[3])
     grams(3, 4, 0)
     reduce_start(0, 0, gbuf, gres[...])
     rest = operator(v.at[3], 4, finish_next(4), None)
@@ -459,9 +495,9 @@
     last = placed(last[0:8], 48) + placed(last[8:16], 64)
     reduce_start(0, 1, fbuf, last)
     reduce_start(1, 0, gbuf, reduce_done(0, 0, gbuf))
-    rest()
     reduce_start(1, 1, fbuf, reduce_done(0, 1, fbuf))
     reduce_start(2, 0, gbuf, reduce_done(1, 0, gbuf))
+    rest()
     for j in range(5):
         high, low = split(jnp.concatenate(grouped(v[j]), 1))
         fhigh[128 * j : 128 * j + 128, :] = high

time: 111 us -> 104 us (0.937)
  Pallas kernels: 107 us -> 101 us
    pallas_call x1, Pallas kernels: 107 us -> 101 us  [on_device(): pl.pallas_call(functools.partial(kernel, nx, ny), out_shape=(block, block...]
where the time goes in v3:
time: 104 us
  Pallas kernels  101 us (97%)
  local copies, waits for them, and re-layouts  2.74 us (3%)
    pallas_call x1, Pallas kernels, on_device(): pl.pallas_call(functools.partial(kernel, nx, ny), out_shape=(block, block...  101 us
    unnamed x4, local copies, waits for them, and re-layouts  2.74 us

profile of v3, /device:TPU:1, one launch (start us, length us, event | category | flops | bytes accessed | tf_op | source)
XLA Modules:
  0.0 103.9 jit_solution(1858355872421340158)
XLA Ops:
  0.6 100.6 %shard_map.86 = (f32[8,2,64,128]{3,2,1,0:T(8,128)}, f32[8,2,64,128]{3,2,1,0:T(8,128)}) custom-call(f32[8,2,64,128]{3,2,1,0:T(8,128)} %bitcast.9, s32[64,128]{1,0:T(8,128)} %bitcast.12, s32[1,128]{1,0:T(1,128)} %bitcast.13, f32[8]{0:T(128)} %ms_in.1, f32[125,125]{1,0:T(8,128)} %kin_in.1, bf16[128,128]{1,0:T(8,128)(2,1)} %constant.4.clone.order_in, ...), custom_call_target="tpu_custom_call" | custom-call | tf_op jit(solution)/shard_map/pallas_call | solution.py:572
  101.2 0.0 copy-start
  101.2 1.9 %copy.13 = f32[16,1,1,64,128]{4,3,2,1,0:T(8,128)} copy(f32[16,1,1,64,128]{4,3,2,1,0:T(8,128)} %bitcast.11) | data formatting | bytes 1048576
  103.1 0.0 copy-done
  103.2 0.8 copy.14
Async XLA Ops:
  101.2 2.0 %copy-start = (f32[8,2,64,128]{3,2,1,0:T(8,128)S(1)}, f32[8,2,64,128]{3,2,1,0:T(8,128)}, u32[]{:S(2)}) copy-start(f32[8,2,64,128]{3,2,1,0:T(8,128)} %get-tuple-element.5) | copy-start | bytes 1572868

commit v4 on v3

--- a/solution.py
+++ b/solution.py
@@ -98,11 +98,11 @@
 def kernel(
     nx, ny,
     x0_in, lab_in, mat_in, ms_in, kin_in, order_in, table_in,
-    xo, ro,
-    x0, lab, mat, ms, kin, order, table,
+    xo_out, ro_out,
+    xo, ro, x0, lab, mat, ms, kin, order, table,
     v, w, rim, corner, ysend, csend, zs, zcs, zr, zcr, tail, zct, kpad, kk, klo, maskb, srow,
     gbuf, fbuf, gm, yst, gres, colr, fhigh, flow,
-    es, er, rs, rr, ss, sr, ins,
+    es, er, rs, rr, ss, sr, ins, outs,
 ):
     fetches = [
         pltpu.make_async_copy(src, dst, ins.at[n])
@@ -332,20 +332,8 @@
                 w[q, j, 16 * a : 16 * a + 4, :] += zr[q, j, 16 + 4 * a : 20 + 4 * a, :]
             w[q, j, 0:4, :] += zcr[q, 4 * j : 4 * j + 4, :]
 
-    def operator(src, number, finish, target):
-        def apply(q, carry):
-            extend_arrived(src, q)
-            if number > 0:
-                return_sent(q)
-            cells(src, q)
-            return_start(q)
-            return carry
-
-        lax.fori_loop(0, NQ, apply, 0)
-        return functools.partial(_finish, src, number, finish, target)
-
-    def operate(src, number, finish, target):
-        lag = NQ - 2
+    def operate(src, number, finish, target, between=None, after=None):
+        lag = NQ - 4
 
         def apply(q):
             extend_arrived(src, q)
@@ -359,7 +347,8 @@
             extend_sent(src, q)
             gather_rims(q)
             finish(q)
-            extend_start(target, q)
+            if target is not None:
+                extend_start(target, q)
 
         def lead(q, carry):
             apply(q)
@@ -375,20 +364,14 @@
             return carry
 
         lax.fori_loop(0, lag, lead, 0)
-        lax.fori_loop(lag, NQ, both, 0)
-        lax.fori_loop(NQ - lag, NQ, trail, 0)
-
-    def _finish(src, number, finish, target):
-        def done(q, carry):
-            return_arrived(q)
-            extend_sent(src, q)
-            gather_rims(q)
-            finish(q)
-            if number < 4:
-                extend_start(target, q)
-            return carry
-
-        lax.fori_loop(0, NQ, done, 0)
+        if between is None:
+            lax.fori_loop(lag, NQ, both, 0)
+            lax.fori_loop(NQ - lag, NQ, trail, 0)
+        else:
+            between()
+            lax.fori_loop(lag, NQ, lead, 0)
+            after()
+            lax.fori_loop(0, NQ, trail, 0)
 
     def reduce_start(stage, number, buf, value):
         start, size, pos, device = stages[stage]
@@ -486,23 +469,20 @@
     operate(v.at[2], 3, finish_next(3), v.at[3])
     grams(3, 4, 0)
     reduce_start(0, 0, gbuf, gres[...])
-    rest = operator(v.at[3], 4, finish_next(4), None)
-
-    last = block(
-        stacked(grouped(v[3]) + grouped(rim[...]) + grouped(tail[...])),
-        stacked(grouped(w[...]) + grouped(zs[...]) + grouped(zct[...])),
-    )
-    last = placed(last[0:8], 48) + placed(last[8:16], 64)
-    reduce_start(0, 1, fbuf, last)
-    reduce_start(1, 0, gbuf, reduce_done(0, 0, gbuf))
-    reduce_start(1, 1, fbuf, reduce_done(0, 1, fbuf))
-    reduce_start(2, 0, gbuf, reduce_done(1, 0, gbuf))
-    rest()
-    for j in range(5):
-        high, low = split(jnp.concatenate(grouped(v[j]), 1))
-        fhigh[128 * j : 128 * j + 128, :] = high
-        flow[128 * j : 128 * j + 128, :] = low
-    reduce_start(2, 1, fbuf, reduce_done(1, 1, fbuf))
+
+    def between():
+        reduce_start(1, 0, gbuf, reduce_done(0, 0, gbuf))
+
+    def after():
+        last = block(
+            stacked(grouped(v[3]) + grouped(rim[...]) + grouped(tail[...])),
+            stacked(grouped(w[...]) + grouped(zs[...]) + grouped(zct[...])),
+        )
+        reduce_start(0, 1, fbuf, placed(last[0:8], 48) + placed(last[8:16], 64))
+        reduce_start(2, 0, gbuf, reduce_done(1, 0, gbuf))
+        reduce_start(1, 1, fbuf, reduce_done(0, 1, fbuf))
+
+    operate(v.at[3], 4, finish_next(4), None, between, after)
 
     theta, delta = colr[0:1, :], colr[1:2, :]
     parts = exact_dot(reduce_done(2, 0, gbuf), table[...])
@@ -520,7 +500,13 @@
         gm[...] = jnp.where(iota((64, 128), 0) == k, row, value - col * row)
         return carry
 
-    lax.fori_loop(0, 48, eliminate, 0)
+    lax.fori_loop(0, 16, eliminate, 0)
+    reduce_start(2, 1, fbuf, reduce_done(1, 1, fbuf))
+    lax.fori_loop(16, 48, eliminate, 0)
+    for j in range(5):
+        high, low = split(jnp.concatenate(grouped(v[j]), 1))
+        fhigh[128 * j : 128 * j + 128, :] = high
+        flow[128 * j : 128 * j + 128, :] = low
     last = reduce_done(2, 1, fbuf)
     inside = (iota((8, 128), 1) >= 48) & (iota((8, 128), 1) < 64)
     gm[48:56, :] += jnp.where(inside, last, 0.0)
@@ -551,6 +537,7 @@
 
     chigh, clow = split(coef)
     chigh, clow = wide(chigh), wide(clow)
+    stores = []
     for pair in range(4):
         at = slice(256 * pair, 256 * pair + 256)
         high, low = fhigh[:, at], flow[:, at]
@@ -559,22 +546,29 @@
             one = out[:, 128 * (g - 2 * pair) : 128 * (g - 2 * pair) + 128]
             xo[:, :, 8 * g : 8 * g + 8, :] = x0[:, :, 8 * g : 8 * g + 8, :] + one[0:128].reshape(NQ, CQ, 8, 128)
             ro[:, :, 8 * g : 8 * g + 8, :] = one[128:256].reshape(NQ, CQ, 8, 128)
+        rows = pl.ds(16 * pair, 16)
+        for n, (src, dst) in enumerate(((xo, xo_out), (ro, ro_out))):
+            stores.append(pltpu.make_async_copy(src.at[:, :, rows, :], dst.at[:, :, rows, :], outs.at[n, pair]))
+            stores[-1].start()
 
     for q in range(NQ):
         return_sent(q)
+    for store in stores:
+        store.wait()
 
 
 def on_device(start_block, labels, materials, mat_scales, cell_stiffness):
     nx, ny = lax.axis_size("gx"), lax.axis_size("gy")
     slots = 8 + ny // 4 + nx // 2
-    vmem = pl.BlockSpec(memory_space=pltpu.VMEM)
     block = jax.ShapeDtypeStruct((NQ, CQ, 64, 128), F32)
     out = pl.pallas_call(
         functools.partial(kernel, nx, ny),
-        out_shape=(block, block),
+        out_shape=[block, block],
         in_specs=[pl.BlockSpec(memory_space=pltpu.HBM)] * 7,
-        out_specs=(vmem, vmem),
+        out_specs=[pl.BlockSpec(memory_space=pltpu.HBM)] * 2,
         scratch_shapes=[
+            pltpu.VMEM((NQ, CQ, 64, 128), F32),
+            pltpu.VMEM((NQ, CQ, 64, 128), F32),
             pltpu.VMEM((NQ, CQ, 64, 128), F32),
             pltpu.VMEM((64, 128), jnp.int32),
             pltpu.VMEM((1, 128), jnp.int32),
@@ -614,6 +608,7 @@
             pltpu.SemaphoreType.DMA((2, slots)),
             pltpu.SemaphoreType.DMA((2, slots)),
             pltpu.SemaphoreType.DMA((7,)),
+            pltpu.SemaphoreType.DMA((2, 4)),
         ],
         compiler_params=pltpu.CompilerParams(
             collective_id=0, has_side_effects=True, vmem_limit_bytes=56 * 1024 * 1024

time: 104 us -> 103 us (level)
  Pallas kernels: 101 us -> 99.1 us
    pallas_call x1, Pallas kernels: 101 us -> 99.1 us  [on_device(): pl.pallas_call(functools.partial(kernel, nx, ny), out_shape=[block, block...]
where the time goes in v4:
time: 103 us; the launch traced here: 102 us
  Pallas kernels  99.1 us (96%)
  local copies, waits for them, and re-layouts  2.74 us (3%)
    pallas_call x1, Pallas kernels, on_device(): pl.pallas_call(functools.partial(kernel, nx, ny), out_shape=[block, block...  99.1 us
    unnamed x4, local copies, waits for them, and re-layouts  2.74 us

profile of v4, /device:TPU:1, one launch (start us, length us, event | category | flops | bytes accessed | tf_op | source)
XLA Modules:
  0.0 102.4 jit_solution(9229938354610074878)
XLA Ops:
  0.6 99.1 %shard_map.86 = (f32[8,2,64,128]{3,2,1,0:T(8,128)}, f32[8,2,64,128]{3,2,1,0:T(8,128)}) custom-call(f32[8,2,64,128]{3,2,1,0:T(8,128)} %bitcast.9, s32[64,128]{1,0:T(8,128)} %bitcast.12, s32[1,128]{1,0:T(1,128)} %bitcast.13, f32[8]{0:T(128)} %ms_in.1, f32[125,125]{1,0:T(8,128)} %kin_in.1, bf16[128,128]{1,0:T(8,128)(2,1)} %constant.4.clone.order_in, ...), custom_call_target="tpu_custom_call" | custom-call | tf_op jit(solution)/shard_map/pallas_call | solution.py:564
  99.7 0.0 copy-start
  99.7 1.9 %copy.13 = f32[16,1,1,64,128]{4,3,2,1,0:T(8,128)} copy(f32[16,1,1,64,128]{4,3,2,1,0:T(8,128)} %bitcast.11) | data formatting | bytes 1048576
  101.6 0.0 copy-done
  101.6 0.8 copy.14
Async XLA Ops:
  99.7 2.0 %copy-start = (f32[8,2,64,128]{3,2,1,0:T(8,128)S(1)}, f32[8,2,64,128]{3,2,1,0:T(8,128)}, u32[]{:S(2)}) copy-start(f32[8,2,64,128]{3,2,1,0:T(8,128)} %get-tuple-element.5) | copy-start | bytes 1572868

commit v5 on v4

--- a/solution.py
+++ b/solution.py
@@ -537,11 +537,13 @@
 
     chigh, clow = split(coef)
     chigh, clow = wide(chigh), wide(clow)
+    cboth = jnp.concatenate([chigh, clow], 0)
     stores = []
     for pair in range(4):
         at = slice(256 * pair, 256 * pair + 256)
         high, low = fhigh[:, at], flow[:, at]
-        out = dot(chigh, high) + dot(chigh, low) + dot(clow, high)
+        both = dot(cboth, high)
+        out = both[0:256] + both[256:512] + dot(chigh, low)
         for g in (2 * pair, 2 * pair + 1):
             one = out[:, 128 * (g - 2 * pair) : 128 * (g - 2 * pair) + 128]
             xo[:, :, 8 * g : 8 * g + 8, :] = x0[:, :, 8 * g : 8 * g + 8, :] + one[0:128].reshape(NQ, CQ, 8, 128)

time: 103 us -> 103 us (level)
  no operation moved by 1% of the time
where the time goes in v5:
time: 103 us; the launch traced here: 102 us
  Pallas kernels  99.1 us (96%)
  local copies, waits for them, and re-layouts  2.74 us (3%)
    pallas_call x1, Pallas kernels, on_device(): pl.pallas_call(functools.partial(kernel, nx, ny), out_shape=[block, block...  99.1 us
    unnamed x4, local copies, waits for them, and re-layouts  2.74 us

profile of v5, /device:TPU:1, one launch (start us, length us, event | category | flops | bytes accessed | tf_op | source)
XLA Modules:
  0.0 102.5 jit_solution(8574835659962182090)
XLA Ops:
  0.6 99.1 %shard_map.86 = (f32[8,2,64,128]{3,2,1,0:T(8,128)}, f32[8,2,64,128]{3,2,1,0:T(8,128)}) custom-call(f32[8,2,64,128]{3,2,1,0:T(8,128)} %bitcast.9, s32[64,128]{1,0:T(8,128)} %bitcast.12, s32[1,128]{1,0:T(1,128)} %bitcast.13, f32[8]{0:T(128)} %ms_in.1, f32[125,125]{1,0:T(8,128)} %kin_in.1, bf16[128,128]{1,0:T(8,128)(2,1)} %constant.4.clone.order_in, ...), custom_call_target="tpu_custom_call" | custom-call | tf_op jit(solution)/shard_map/pallas_call | solution.py:566
  99.7 0.0 copy-start
  99.7 1.9 %copy.13 = f32[16,1,1,64,128]{4,3,2,1,0:T(8,128)} copy(f32[16,1,1,64,128]{4,3,2,1,0:T(8,128)} %bitcast.11) | data formatting | bytes 1048576
  101.7 0.0 copy-done
  101.7 0.8 copy.14
Async XLA Ops:
  99.7 2.0 %copy-start = (f32[8,2,64,128]{3,2,1,0:T(8,128)S(1)}, f32[8,2,64,128]{3,2,1,0:T(8,128)}, u32[]{:S(2)}) copy-start(f32[8,2,64,128]{3,2,1,0:T(8,128)} %get-tuple-element.5) | copy-start | bytes 1572868
